TPU v7x, 32 devices: a whole 2x2x4 slice. The times are simulated.
32 devices in a mesh: blk: 4 (over y, x), group: 8 (over z, core).
Axes of the slice: x: 2, y: 2, z: 4, core: 2. Of those that a mesh axis runs over, the one named last changes fastest.
Arguments:
- walk_rows: bfloat16 [2048, 32768], P('blk', 'group'), may hold values from -6 to 6
- col_values: bfloat16 [12288, 2048], P('group', 'blk'), may hold values from -0.0546875 to 0.0546875
- col_index: int32 [24, 4], P('group'), may hold values from 0 to 7
- col_count: int32 [8, 4], P('group'), may hold values from 1 to 3, as said below
Outputs:
- inflated: float32 [2048, 2048], P(('blk', 'group'))
Inputs may be any that keep to these rules, and one draw needn't show every extreme that they name: `col_count`: each list holds 1 to 3 valid slots; some list holds 3; contents of the other slots are arbitrary.
All inputs are finite; a program needn't handle non-finite values.
Results may differ from a plain program's by a relative error of at most 0.0003.
Values may be sent and summed in bfloat16 or wider, within the bound.
A program may use at most 64 MiB of HBM per device.

v0:
```python
import jax
import jax.numpy as jnp
from jax import lax
from jax.sharding import PartitionSpec as P


def shifted(shard, axis, by):
    size = lax.axis_size(axis)
    return lax.ppermute(shard, axis, [(i, (i + by) % size) for i in range(size)])


def add_block(total, block, piece):
    return total + jnp.dot(block, piece, preferred_element_type=jnp.float32)


def on_device(walk_rows, col_values, col_index, col_count):
    width = col_values.shape[1]
    slots = col_values.shape[0] // width
    nblock = lax.axis_size("blk")
    myself = lax.axis_index("blk")
    rows_here = walk_rows.shape[0]
    share = rows_here // lax.axis_size("group")

    def panel_product(rows, values, panel):
        index = lax.dynamic_slice_in_dim(col_index, panel, 1, 1)[:, 0]
        count = lax.dynamic_slice_in_dim(col_count, panel, 1, 1)[0, 0]
        total = jnp.zeros((rows.shape[0], width), jnp.float32)
        for slot in range(slots):
            block = lax.dynamic_slice_in_dim(rows, index[slot] * width, width, 1)
            piece = values[slot * width : (slot + 1) * width]
            total = lax.cond(
                slot < count, lambda t, b=block, p=piece: add_block(t, b, p), lambda t: t, total
            )
        return total

    def turn(step, carry):
        values, result = carry
        panel = (myself - step) % nblock
        part = panel_product(walk_rows, values, panel)
        reduced = lax.psum_scatter(part, "group", scatter_dimension=0, tiled=True)
        result = lax.dynamic_update_slice_in_dim(result, reduced, panel * width, 1)
        values = shifted(values, "blk", 1)
        return (values, result)

    start_out = jnp.zeros((share, nblock * width), jnp.float32)
    unused, expanded = lax.fori_loop(0, nblock, turn, (col_values, start_out))
    squared = expanded * expanded
    column = jnp.sum(squared, axis=0)
    total = lax.psum(column, ("blk", "group"))
    scale = total / (nblock * rows_here) + 1e-06
    return squared / scale


def solution(mesh):
    return jax.shard_map(
        on_device,
        mesh=mesh,
        in_specs=(P("blk", "group"), P("group", "blk"), P("group", None), P("group", None)),
        out_specs=P(("blk", "group"), None),
        check_vma=False,
    )
```

profile of v0, /device:TPU:0, one launch (start us, length us, event | category | flops | bytes accessed | tf_op | source)
XLA Modules:
  0.0 247.3 jit_solution(2922820204925727961)
XLA Ops:
  6.5 2.7 %copy.23 = bf16[1536,512]{1,0:T(8,128)(2,1)} copy(bf16[1536,512]{1,0:T(8,128)(2,1)} %param.13) | data formatting | bytes 3145728
  9.2 0.1 copy.5
  9.4 190.8 %while.17 = (s32[]{:T(128)}, bf16[1536,512]{1,0:T(8,128)(2,1)}, f32[64,2048]{1,0:T(8,128)S(1)}, s32[]{:T(128)}, s32[1,4]{1,0:T(1,128)S(1)}, /*index=5*/s32[3,4]{...) while((s32[]{:T(128)}, bf16[1536,512]{1,0:T(8,128)(2,1)}, ...), condition=%wide.region_8.9_spmd, body=%wide.region_0.8_spmd.sunk | while | flops 805830656 | bytes 25822076 | solution.py:46
  9.4 0.0 reduce-scatter.2.cloned.1.call-start
  9.5 0.6 fusion.14
  11.9 0.6 fusion.15
  13.8 1.4 copy.17
  15.2 1.6 conditional.6
  15.2 1.6 fusion.3
  16.8 1.0 copy-done
  17.8 0.0 reduce-scatter.2.cloned.1.call-update
  17.8 3.0 %collective-permute-start = (bf16[1536,512]{1,0:T(8,128)(2,1)S(1)}, bf16[1536,512]{1,0:T(8,128)(2,1)}, u32[]{:S(2)}, u32[]{:S(2)}) collective-permute-start(bf16[1536,512]{1,0:T(8,128)(2,1)S(1)} %copy.17), channel_id=1, source_target_pairs={{0,8},{8,16},{16,24},{24,0},{1,9},{9,17},{17,25},{25,1},{2,10},{10... | collective-permute-start | bytes 4718600 | tf_op jit(solution)/shard_map/while/body/eval_jaxpr/ppermute | solution.py:9
  20.8 36.2 %reduce-scatter.2.cloned.1.call-done = f32[64,512]{1,0:T(8,128)} async-done(((f32[512,512]{1,0:T(8,128)}), f32[64,512]{1,0:T(8,128)}) %reduce-scatter.2.cloned.1.call-update) | async-done | bytes 131088 | tf_op jit(solution)/shard_map/while/body/eval_jaxpr/reduce_scatter | solution.py:40
  57.0 0.9 constant_dynamic-update-slice_fusion.2
  57.9 0.0 reduce-scatter.2.cloned.1.call-start
  58.0 0.6 fusion.14
  60.5 0.6 fusion.15
  62.3 1.4 copy.17
  63.7 1.6 conditional.6
  63.7 1.6 fusion.3
  65.4 1.0 copy-done
  66.3 0.0 reduce-scatter.2.cloned.1.call-update
  66.4 1.6 collective-permute-start
  68.0 37.9 %reduce-scatter.2.cloned.1.call-done = f32[64,512]{1,0:T(8,128)} async-done(((f32[512,512]{1,0:T(8,128)}), f32[64,512]{1,0:T(8,128)}) %reduce-scatter.2.cloned.1.call-update) | async-done | bytes 131088 | tf_op jit(solution)/shard_map/while/body/eval_jaxpr/reduce_scatter | solution.py:40
  105.8 0.9 constant_dynamic-update-slice_fusion.2
  106.8 0.0 reduce-scatter.2.cloned.1.call-start
  106.9 0.6 fusion.14
  109.3 0.6 fusion.15
  111.2 1.4 copy.17
  112.6 1.6 conditional.6
  112.6 1.6 fusion.3
  114.2 1.0 copy-done
  115.2 1.8 collective-permute-start
  117.0 35.1 %reduce-scatter.2.cloned.1.call-done = f32[64,512]{1,0:T(8,128)} async-done(((f32[512,512]{1,0:T(8,128)}), f32[64,512]{1,0:T(8,128)}) %reduce-scatter.2.cloned.1.call-update) | async-done | bytes 131088 | tf_op jit(solution)/shard_map/while/body/eval_jaxpr/reduce_scatter | solution.py:40
  152.1 0.9 constant_dynamic-update-slice_fusion.2
  153.0 0.0 reduce-scatter.2.cloned.1.call-start
  153.1 0.6 fusion.14
  155.6 0.6 fusion.15
  157.4 1.4 copy.17
  158.9 1.6 conditional.6
  158.9 1.6 fusion.3
  160.5 1.0 copy-done
  161.5 1.8 collective-permute-start
  163.3 35.9 %reduce-scatter.2.cloned.1.call-done = f32[64,512]{1,0:T(8,128)} async-done(((f32[512,512]{1,0:T(8,128)}), f32[64,512]{1,0:T(8,128)}) %reduce-scatter.2.cloned.1.call-update) | async-done | bytes 131088 | tf_op jit(solution)/shard_map/while/body/eval_jaxpr/reduce_scatter | solution.py:40
  199.2 0.9 constant_dynamic-update-slice_fusion.2
  200.1 0.1 multiply_reduce_fusion
  200.2 39.7 %psum.7 = f32[2048]{0:T(1024)S(1)} all-reduce(f32[2048]{0:T(1024)S(1)} %multiply_reduce_fusion), channel_id=1, replica_groups=mesh['blk'=4,'group'=8] {'blk','group'}, use_global_device_ids=true, to_apply=%region_10.11 | all-reduce | flops 2048 | bytes 16384 | tf_op jit(solution)/shard_map/psum | solution.py:49
  239.9 0.8 multiply_divide_fusion
  (28 shorter events, 0.2 us)
Async XLA Ops:
  6.5 2.7 %copy-start.2 = (s32[3,4]{1,0:T(4,128)S(1)}, s32[3,4]{1,0:T(4,128)}, u32[]{:S(2)}) copy-start(s32[3,4]{1,0:T(4,128)} %param.14) | copy-start | bytes 148
  6.5 2.8 %copy-start.1 = (s32[1,4]{1,0:T(1,128)S(1)}, s32[1,4]{1,0:T(1,128)}, u32[]{:S(2)}) copy-start(s32[1,4]{1,0:T(1,128)} %param.15) | copy-start | bytes 52
  9.4 47.6 %reduce-scatter.2.cloned.1.call-start = ((), (), s32[]{:S(2)}) async-start(), calls=%async_computation.1 | async-start | bytes 1179648 | tf_op jit(solution)/shard_map/while/body/eval_jaxpr/reduce_scatter | solution.py:40
  16.8 1.0 copy-start
  17.8 40.1 %collective-permute-start = (bf16[1536,512]{1,0:T(8,128)(2,1)S(1)}, bf16[1536,512]{1,0:T(8,128)(2,1)}, u32[]{:S(2)}, u32[]{:S(2)}) collective-permute-start(bf16[1536,512]{1,0:T(8,128)(2,1)S(1)} %copy.17), channel_id=1, source_target_pairs={{0,8},{8,16},{16,24},{24,0},{1,9},{9,17},{17,25},{25,1},{2,10},{10... | collective-permute-start | bytes 4718600 | tf_op jit(solution)/shard_map/while/body/eval_jaxpr/ppermute | solution.py:9
  57.9 47.9 %reduce-scatter.2.cloned.1.call-start = ((), (), s32[]{:S(2)}) async-start(), calls=%async_computation.1 | async-start | bytes 1179648 | tf_op jit(solution)/shard_map/while/body/eval_jaxpr/reduce_scatter | solution.py:40
  65.4 1.0 copy-start
  66.4 40.4 %collective-permute-start = (bf16[1536,512]{1,0:T(8,128)(2,1)S(1)}, bf16[1536,512]{1,0:T(8,128)(2,1)}, u32[]{:S(2)}, u32[]{:S(2)}) collective-permute-start(bf16[1536,512]{1,0:T(8,128)(2,1)S(1)} %copy.17), channel_id=1, source_target_pairs={{0,8},{8,16},{16,24},{24,0},{1,9},{9,17},{17,25},{25,1},{2,10},{10... | collective-permute-start | bytes 4718600 | tf_op jit(solution)/shard_map/while/body/eval_jaxpr/ppermute | solution.py:9
  106.8 45.3 %reduce-scatter.2.cloned.1.call-start = ((), (), s32[]{:S(2)}) async-start(), calls=%async_computation.1 | async-start | bytes 1179648 | tf_op jit(solution)/shard_map/while/body/eval_jaxpr/reduce_scatter | solution.py:40
  114.2 1.0 copy-start
  115.2 37.8 %collective-permute-start = (bf16[1536,512]{1,0:T(8,128)(2,1)S(1)}, bf16[1536,512]{1,0:T(8,128)(2,1)}, u32[]{:S(2)}, u32[]{:S(2)}) collective-permute-start(bf16[1536,512]{1,0:T(8,128)(2,1)S(1)} %copy.17), channel_id=1, source_target_pairs={{0,8},{8,16},{16,24},{24,0},{1,9},{9,17},{17,25},{25,1},{2,10},{10... | collective-permute-start | bytes 4718600 | tf_op jit(solution)/shard_map/while/body/eval_jaxpr/ppermute | solution.py:9
  153.0 46.2 %reduce-scatter.2.cloned.1.call-start = ((), (), s32[]{:S(2)}) async-start(), calls=%async_computation.1 | async-start | bytes 1179648 | tf_op jit(solution)/shard_map/while/body/eval_jaxpr/reduce_scatter | solution.py:40
  160.5 1.0 copy-start
  161.5 38.7 %collective-permute-start = (bf16[1536,512]{1,0:T(8,128)(2,1)S(1)}, bf16[1536,512]{1,0:T(8,128)(2,1)}, u32[]{:S(2)}, u32[]{:S(2)}) collective-permute-start(bf16[1536,512]{1,0:T(8,128)(2,1)S(1)} %copy.17), channel_id=1, source_target_pairs={{0,8},{8,16},{16,24},{24,0},{1,9},{9,17},{17,25},{25,1},{2,10},{10... | collective-permute-start | bytes 4718600 | tf_op jit(solution)/shard_map/while/body/eval_jaxpr/ppermute | solution.py:9
Sparse Core Ops, SparseCore 0:
  17.9 39.0 reduce-scatter.1
  66.5 39.2 reduce-scatter.1
  115.3 36.7 reduce-scatter.1
  161.6 37.5 reduce-scatter.1
where the time goes:
time: 248 us; the launch traced here: 247 us
  waiting for transfers between devices  145 us (58%)
  blocking collectives  39.7 us (16%)
  local copies, waits for them, and re-layouts  18.5 us (7%)
  between operations  13.1 us (5%)
  loops' own time  12.8 us (5%)
  starting transfers between devices  8.39 us (3%)
  matrix products  6.32 us (3%)
  other arithmetic  3.37 us (1%)
    reduce_scatter x4, waiting for transfers between devices, turn(): reduced = lax.psum_scatter(part, 'group', scatter_dimension=0, tiled=True)  145 us
    psum x1, blocking collectives, on_device(): total = lax.psum(column, ('blk', 'group'))  39.7 us
    another operation x1, loops' own time, on_device(): unused, expanded = lax.fori_loop(0, nblock, turn, (col_values, start_out))  12.7 us
    ppermute x4, starting transfers between devices, shifted(): lax.ppermute(shard, axis, [(i, (i + by) % size) for i in range(size)])  8.23 us
    dot_general x4, matrix products, add_block(): return total + jnp.dot(block, piece, preferred_element_type=jnp.float32)  6.32 us
    another operation x4, local copies, waits for them, and re-layouts  5.64 us
  transfers between devices with their start and end apart: 8, of which 4 were waited for; matrix products, arithmetic and copies ran while one was open for 1% of the time, Pallas kernels for 0%

commit v1 on v0

v1 whole, which is shorter than its diff:
```python
import functools

import jax
import jax.numpy as jnp
from jax import lax
from jax.experimental import pallas as pl
from jax.experimental.pallas import tpu as pltpu
from jax.sharding import PartitionSpec as P

CHUNKS = 4
LAG = 3


def snake(i, n):
    half = n // 2
    return jnp.where(i < half, i, half + n - 1 - i)


def kernel(n, ng, a_hbm, b_hbm, idx_ref, cnt_ref, sq_ref, scale_ref,
           a_v, gath, part, sib, summed, zin, stat, stat2, gin, bin_,
           a_sem, b_sem, bs_sem, br_sem, xs_sem, xr_sem, zs_sem, zr_sem, s_sem):
    rows, width, nc = a_hbm.shape[0], b_hbm.shape[1], gath.shape[1]
    slots = b_hbm.shape[0] // width
    inner = a_hbm.shape[1] // width
    cw = width // nc
    share, nz = rows // ng, ng // 2
    units = n * nc
    me_b, me_g = lax.axis_index("blk"), lax.axis_index("group")
    core, z = me_g % 2, me_g // 2
    pos = snake(me_b, n)
    ring = (snake((pos + 1) % n, n), snake((pos + n - 1) % n, n))

    def b_copy(c):
        return pltpu.make_async_copy(
            b_hbm.at[:, pl.ds(pl.multiple_of(c * cw, cw), cw)], gath.at[me_b, c], b_sem.at[c])

    for c in range(nc):
        b_copy(c).start()
    for k in range(inner):
        pltpu.make_async_copy(a_hbm.at[:, k * width:(k + 1) * width], a_v.at[k], a_sem).start()

    barrier = pltpu.get_barrier_semaphore()

    @pl.loop(1, ng)
    def _(d):
        pl.semaphore_signal(barrier, inc=1, device_id={"group": (me_g + d) % ng},
                            device_id_type=pl.DeviceIdType.MESH)

    @pl.loop(1, n)
    def _(d):
        pl.semaphore_signal(barrier, inc=1, device_id={"blk": (me_b + d) % n},
                            device_id_type=pl.DeviceIdType.MESH)

    pl.semaphore_wait(barrier, ng - 1 + n - 1)

    def ring_copy(panel, c, d):
        to = ring[d] if isinstance(d, int) else jnp.where(d == 0, ring[0], ring[1])
        return pltpu.make_async_remote_copy(
            src_ref=gath.at[panel, c], dst_ref=gath.at[panel, c],
            send_sem=bs_sem.at[d, panel, c], recv_sem=br_sem.at[panel, c],
            device_id={"blk": to}, device_id_type=pl.DeviceIdType.MESH)

    def goes_on(hop, c, d):
        return (hop + 1 < n // 2) | ((hop + 1 == n // 2) & (c % 2 == d))

    def unit(t):
        u = t - nc
        own = t < nc
        hop = jnp.where(own, 0, 1 + u // (2 * nc))
        r = u % (2 * nc)
        c = jnp.where(own, t, jnp.where(hop == n // 2, r, r // 2))
        d = jnp.where(own, 0, r % 2)
        panel = snake((pos + jnp.where(d == 0, n - hop, hop)) % n, n)
        return hop, c, d, panel

    for c in range(nc):
        b_copy(c).wait()
        for d in range(2):
            if n // 2 > 1 or c % 2 == d:
                ring_copy(me_b, c, d).start()
    pltpu.make_async_copy(a_v, a_v, a_sem).wait()

    def sib_copy(t):
        return pltpu.make_async_remote_copy(
            src_ref=part.at[t, 1 - core], dst_ref=sib.at[t],
            send_sem=xs_sem.at[t], recv_sem=xr_sem.at[t],
            device_id={"group": me_g + 1 - 2 * core}, device_id_type=pl.DeviceIdType.MESH)

    def z_copy(t, d):
        to = (z + d) % nz
        return pltpu.make_async_remote_copy(
            src_ref=summed.at[t, to], dst_ref=zin.at[t, d - 1],
            send_sem=zs_sem.at[t], recv_sem=zr_sem.at[t],
            device_id={"group": to * 2 + core}, device_id_type=pl.DeviceIdType.MESH)

    def first(t):
        hop, c, d, panel = unit(t)

        @pl.when(hop > 0)
        def _():
            ring_copy(panel, c, d).wait_recv()

            @pl.when(goes_on(hop, c, d))
            def _():
                ring_copy(panel, c, d).start()

        total = jnp.zeros((rows, cw), jnp.float32)
        count = jnp.full((1, cw), cnt_ref[0, panel], jnp.int32)
        for s in range(slots):
            k = jnp.maximum(jnp.minimum(idx_ref[s, panel], inner - 1), 0)
            block = a_v[k]
            piece = gath[panel, c, s * width:(s + 1) * width, :]
            product = jnp.dot(block, piece, preferred_element_type=jnp.float32)
            total = total + jnp.where(s < count, product, 0.0)
        for q in range(ng):
            part[t, q % 2, q // 2] = total[q * share:(q + 1) * share]
        sib_copy(t).start()

    def second(t):
        sib_copy(t).wait_recv()
        summed[t] = part[t, core] + sib[t]

        @pl.loop(1, nz)
        def _(d):
            z_copy(t, d).start()

    def third(t):
        hop, c, d, panel = unit(t)
        pltpu.make_async_copy(zin.at[t], zin.at[t], zr_sem.at[t]).wait()
        total = summed[t, z]
        for i in range(nz - 1):
            total = total + zin[t, i]
        squared = total * total
        at = pl.ds(pl.multiple_of(panel * width + c * cw, cw), cw)
        sq_ref[:, at] = squared
        stat[:, at] = jnp.sum(squared, axis=0, keepdims=True)

    @pl.loop(0, units + LAG)
    def _(t):
        @pl.when(t < units)
        def _():
            first(t)

        @pl.when((t >= 1) & (t < units + 1))
        def _():
            second(t - 1)

        @pl.when(t >= LAG)
        def _():
            third(t - LAG)

    def exchange(source, into, axis, me, size, k):
        @pl.loop(1, size)
        def _(d):
            pltpu.make_async_remote_copy(
                src_ref=source, dst_ref=into.at[d - 1], send_sem=s_sem.at[k], recv_sem=s_sem.at[k + 1],
                device_id={axis: (me + d) % size}, device_id_type=pl.DeviceIdType.MESH).start()

        pltpu.make_async_copy(into, into, s_sem.at[k + 1]).wait()

    exchange(stat, gin, "group", me_g, ng, 0)
    stat2[...] = stat[...] + jnp.sum(gin[...], axis=0)
    exchange(stat2, bin_, "blk", me_b, n, 2)
    total = stat2[...] + jnp.sum(bin_[...], axis=0)
    scale_ref[...] = total / (n * rows) + 1e-6

    pltpu.make_async_copy(gin, gin, s_sem.at[0]).wait()
    pltpu.make_async_copy(bin_, bin_, s_sem.at[2]).wait()

    @pl.loop(0, units)
    def _(t):
        sib_copy(t).wait_send()
        pltpu.make_async_copy(zin.at[t], zin.at[t], zs_sem.at[t]).wait()
        hop, c, d, panel = unit(t)
        for way in range(2):
            @pl.when(((hop == 0) | (d == way)) & goes_on(hop, c, way))
            def _():
                ring_copy(panel, c, way).wait_send()


def on_device(walk_rows, col_values, col_index, col_count):
    n, ng = lax.axis_size("blk"), lax.axis_size("group")
    rows, width = walk_rows.shape[0], col_values.shape[1]
    cw, units, share, nz = width // CHUNKS, n * CHUNKS, rows // ng, ng // 2
    cols = n * width
    f32, bf16 = jnp.float32, jnp.bfloat16
    dma = pltpu.SemaphoreType.DMA
    squared, scale = pl.pallas_call(
        functools.partial(kernel, n, ng),
        out_shape=(jax.ShapeDtypeStruct((share, cols), f32), jax.ShapeDtypeStruct((1, cols), f32)),
        in_specs=[pl.BlockSpec(memory_space=pl.ANY)] * 2 + [pl.BlockSpec(memory_space=pltpu.SMEM)] * 2,
        out_specs=(pl.BlockSpec(memory_space=pltpu.VMEM),) * 2,
        scratch_shapes=[
            pltpu.VMEM((walk_rows.shape[1] // width, rows, width), bf16),
            pltpu.VMEM((n, CHUNKS, col_values.shape[0], cw), bf16),
            pltpu.VMEM((units, 2, nz, share, cw), f32),
            pltpu.VMEM((units, nz, share, cw), f32),
            pltpu.VMEM((units, nz, share, cw), f32),
            pltpu.VMEM((units, nz - 1, share, cw), f32),
            pltpu.VMEM((1, cols), f32),
            pltpu.VMEM((1, cols), f32),
            pltpu.VMEM((ng - 1, 1, cols), f32),
            pltpu.VMEM((n - 1, 1, cols), f32),
            dma, dma((CHUNKS,)), dma((2, n, CHUNKS)), dma((n, CHUNKS)),
            dma((units,)), dma((units,)), dma((units,)), dma((units,)), dma((4,)),
        ],
        compiler_params=pltpu.CompilerParams(
            collective_id=0, has_side_effects=True, vmem_limit_bytes=56 * 2**20),
    )(walk_rows, col_values, col_index, col_count)
    return squared / scale


def solution(mesh):
    return jax.shard_map(
        on_device,
        mesh=mesh,
        in_specs=(P("blk", "group"), P("group", "blk"), P("group", None), P("group", None)),
        out_specs=P(("blk", "group"), None),
        check_vma=False,
    )
```

time: 248 us -> 81.1 us (0.33)
  waiting for transfers between devices: 145 us -> 0 us
  Pallas kernels: 0 us -> 79 us
  blocking collectives: 39.7 us -> 0 us
  local copies, waits for them, and re-layouts: 18.5 us -> 0 us
  between operations: 13.1 us -> 0.01 us
  loops' own time: 12.8 us -> 0 us
  starting transfers between devices: 8.39 us -> 0 us
  matrix products: 6.32 us -> 0 us
    reduce_scatter x4 -> x0, waiting for transfers between devices: 145 us -> none  [turn(): reduced = lax.psum_scatter(part, 'group', scatter_dimension=0, tiled=True)]
    pallas_call x0 -> x1, Pallas kernels: none -> 79 us  [on_device(): pl.pallas_call(functools.partial(kernel, n, ng), out_shape=(jax.ShapeDtyp...]
    psum x1 -> x0, blocking collectives: 39.7 us -> none  [on_device(): total = lax.psum(column, ('blk', 'group'))]
    another operation x13 -> x0, loops' own time: 12.8 us -> none  [the longest x1 12.7 us: on_device(): unused, expanded = lax.fori_loop(0, nblock, turn, (col_values, start_out))]
    ppermute x4 -> x0, starting transfers between devices: 8.23 us -> none  [shifted(): lax.ppermute(shard, axis, [(i, (i + by) % size) for i in range(size)])]
    dot_general x4 -> x0, matrix products: 6.32 us -> none  [add_block(): return total + jnp.dot(block, piece, preferred_element_type=jnp.float32)]
    another operation x4 -> x0, local copies, waits for them, and re-layouts: 5.64 us -> none
    while x9 -> x0, local copies, waits for them, and re-layouts: 3.97 us -> none
  transfers between devices with their start and end apart: 8 -> 0, of which waited for: 4 -> 0; matrix products, arithmetic and copies ran while one was open for 1% -> 0% of each run, Pallas kernels for 0% -> 0%
where the time goes in v1:
time: 81.1 us; the launch traced here: 80.9 us
  Pallas kernels  79 us (97%)
  other arithmetic  1.88 us (2%)
    pallas_call x1, Pallas kernels, on_device(): pl.pallas_call(functools.partial(kernel, n, ng), out_shape=(jax.ShapeDtyp...  79 us
    div x1, other arithmetic, on_device(): return squared / scale  1.88 us

profile of v1, /device:TPU:0, one launch (start us, length us, event | category | flops | bytes accessed | tf_op | source)
XLA Modules:
  0.0 80.9 jit_solution(2326366073401856300)
XLA Ops:
  0.0 79.0 %shard_map.46 = (f32[64,2048]{1,0:T(8,128)}, f32[1,2048]{1,0:T(1,128)}) custom-call(bf16[512,4096]{1,0:T(8,128)(2,1)} %a_hbm.1, bf16[1536,512]{1,0:T(8,128)(2,1)} %b_hbm.1, s32[3,4]{1,0:T(4,128)} %idx_ref.1, s32[1,4]{1,0:T(1,128)} %cnt_ref.1), custom_call_target="tpu_custom_call" | custom-call | tf_op jit(solution)/shard_map/pallas_call | solution.py:188
  79.1 1.9 %broadcast_divide_fusion = f32[64,2048]{1,0:T(8,128)} fusion(f32[64,2048]{1,0:T(8,128)} %get-tuple-element.7, f32[2048]{0:T(1024)} %bitcast.1), kind=kLoop, calls=%fused_computation | loop fusion | flops 131072 | bytes 1056768 | tf_op jit(solution)/shard_map/div | solution.py:210

commit v2 on v1

--- a/solution.py
+++ b/solution.py
@@ -18,7 +18,7 @@
 
 def kernel(n, ng, a_hbm, b_hbm, idx_ref, cnt_ref, sq_ref, scale_ref,
            a_v, gath, part, sib, summed, zin, stat, stat2, gin, bin_,
-           a_sem, b_sem, bs_sem, br_sem, xs_sem, xr_sem, zs_sem, zr_sem, s_sem):
+           a_sem, b_sem, bs_sem, br_sem, bh_sem, xs_sem, xr_sem, zs_sem, zr_sem, s_sem):
     rows, width, nc = a_hbm.shape[0], b_hbm.shape[1], gath.shape[1]
     slots = b_hbm.shape[0] // width
     inner = a_hbm.shape[1] // width
@@ -60,8 +60,24 @@
             send_sem=bs_sem.at[d, panel, c], recv_sem=br_sem.at[panel, c],
             device_id={"blk": to}, device_id_type=pl.DeviceIdType.MESH)
 
-    def goes_on(hop, c, d):
-        return (hop + 1 < n // 2) | ((hop + 1 == n // 2) & (c % 2 == d))
+    tall = slots * width // 2
+
+    def half_copy(panel, c, d):
+        part_of = gath.at[panel, c, pl.ds(pl.multiple_of(d * tall, tall), tall)]
+        return pltpu.make_async_remote_copy(
+            src_ref=part_of, dst_ref=part_of,
+            send_sem=bs_sem.at[d, panel, c], recv_sem=bh_sem.at[d, c],
+            device_id={"blk": ring[d] if isinstance(d, int) else jnp.where(d == 0, ring[0], ring[1])},
+            device_id_type=pl.DeviceIdType.MESH)
+
+    def pass_on(panel, hop, c, d, act):
+        @pl.when(hop + 1 < n // 2)
+        def _():
+            act(ring_copy(panel, c, d))
+
+        @pl.when(hop + 1 == n // 2)
+        def _():
+            act(half_copy(panel, c, d))
 
     def unit(t):
         u = t - nc
@@ -76,8 +92,7 @@
     for c in range(nc):
         b_copy(c).wait()
         for d in range(2):
-            if n // 2 > 1 or c % 2 == d:
-                ring_copy(me_b, c, d).start()
+            pass_on(me_b, 0, c, d, lambda copy: copy.start())
     pltpu.make_async_copy(a_v, a_v, a_sem).wait()
 
     def sib_copy(t):
@@ -96,13 +111,15 @@
     def first(t):
         hop, c, d, panel = unit(t)
 
-        @pl.when(hop > 0)
+        @pl.when((hop > 0) & (hop < n // 2))
         def _():
             ring_copy(panel, c, d).wait_recv()
-
-            @pl.when(goes_on(hop, c, d))
-            def _():
-                ring_copy(panel, c, d).start()
+            pass_on(panel, hop, c, d, lambda copy: copy.start())
+
+        @pl.when(hop == n // 2)
+        def _():
+            half_copy(panel, c, 0).wait_recv()
+            half_copy(panel, c, 1).wait_recv()
 
         total = jnp.zeros((rows, cw), jnp.float32)
         count = jnp.full((1, cw), cnt_ref[0, panel], jnp.int32)
@@ -173,9 +190,9 @@
         pltpu.make_async_copy(zin.at[t], zin.at[t], zs_sem.at[t]).wait()
         hop, c, d, panel = unit(t)
         for way in range(2):
-            @pl.when(((hop == 0) | (d == way)) & goes_on(hop, c, way))
+            @pl.when((hop == 0) | (d == way))
             def _():
-                ring_copy(panel, c, way).wait_send()
+                pass_on(panel, hop, c, way, lambda copy: copy.wait_send())
 
 
 def on_device(walk_rows, col_values, col_index, col_count):
@@ -201,7 +218,7 @@
             pltpu.VMEM((1, cols), f32),
             pltpu.VMEM((ng - 1, 1, cols), f32),
             pltpu.VMEM((n - 1, 1, cols), f32),
-            dma, dma((CHUNKS,)), dma((2, n, CHUNKS)), dma((n, CHUNKS)),
+            dma, dma((CHUNKS,)), dma((2, n, CHUNKS)), dma((n, CHUNKS)), dma((2, CHUNKS)),
             dma((units,)), dma((units,)), dma((units,)), dma((units,)), dma((4,)),
         ],
         compiler_params=pltpu.CompilerParams(

time: 81.1 us -> 78.4 us (0.967)
  Pallas kernels: 79 us -> 76.4 us
    pallas_call x1, Pallas kernels: 79 us -> 76.4 us  [on_device(): pl.pallas_call(functools.partial(kernel, n, ng), out_shape=(jax.ShapeDtyp...]
where the time goes in v2:
time: 78.4 us; the launch traced here: 78.2 us
  Pallas kernels  76.4 us (97%)
  other arithmetic  1.88 us (2%)
    pallas_call x1, Pallas kernels, on_device(): pl.pallas_call(functools.partial(kernel, n, ng), out_shape=(jax.ShapeDtyp...  76.4 us
    div x1, other arithmetic, on_device(): return squared / scale  1.88 us

profile of v2, /device:TPU:0, one launch (start us, length us, event | category | flops | bytes accessed | tf_op | source)
XLA Modules:
  0.0 78.2 jit_solution(24395537725042966)
XLA Ops:
  0.0 76.4 %shard_map.46 = (f32[64,2048]{1,0:T(8,128)}, f32[1,2048]{1,0:T(1,128)}) custom-call(bf16[512,4096]{1,0:T(8,128)(2,1)} %a_hbm.1, bf16[1536,512]{1,0:T(8,128)(2,1)} %b_hbm.1, s32[3,4]{1,0:T(4,128)} %idx_ref.1, s32[1,4]{1,0:T(1,128)} %cnt_ref.1), custom_call_target="tpu_custom_call" | custom-call | tf_op jit(solution)/shard_map/pallas_call | solution.py:205
  76.4 1.9 %broadcast_divide_fusion = f32[64,2048]{1,0:T(8,128)} fusion(f32[64,2048]{1,0:T(8,128)} %get-tuple-element.7, f32[2048]{0:T(1024)} %bitcast.1), kind=kLoop, calls=%fused_computation | loop fusion | flops 131072 | bytes 1056768 | tf_op jit(solution)/shard_map/div | solution.py:227

commit v3 on v2

--- a/solution.py
+++ b/solution.py
@@ -158,9 +158,13 @@
         def _():
             first(t)
 
-        @pl.when((t >= 1) & (t < units + 1))
+        @pl.when((t >= 1) & (t < units - nc + 1))
         def _():
             second(t - 1)
+
+        @pl.when((t >= units - nc) & (t < units))
+        def _():
+            second(t)
 
         @pl.when(t >= LAG)
         def _():

time: 78.4 us -> 76.7 us (0.978)
  Pallas kernels: 76.4 us -> 74.7 us
    pallas_call x1, Pallas kernels: 76.4 us -> 74.7 us  [on_device(): pl.pallas_call(functools.partial(kernel, n, ng), out_shape=(jax.ShapeDtyp...]
where the time goes in v3:
time: 76.7 us; the launch traced here: 76.6 us
  Pallas kernels  74.7 us (97%)
  other arithmetic  1.88 us (2%)
    pallas_call x1, Pallas kernels, on_device(): pl.pallas_call(functools.partial(kernel, n, ng), out_shape=(jax.ShapeDtyp...  74.7 us
    div x1, other arithmetic, on_device(): return squared / scale  1.88 us

profile of v3, /device:TPU:0, one launch (start us, length us, event | category | flops | bytes accessed | tf_op | source)
XLA Modules:
  0.0 76.6 jit_solution(10159469800697534653)
XLA Ops:
  0.0 74.7 %shard_map.46 = (f32[64,2048]{1,0:T(8,128)}, f32[1,2048]{1,0:T(1,128)}) custom-call(bf16[512,4096]{1,0:T(8,128)(2,1)} %a_hbm.1, bf16[1536,512]{1,0:T(8,128)(2,1)} %b_hbm.1, s32[3,4]{1,0:T(4,128)} %idx_ref.1, s32[1,4]{1,0:T(1,128)} %cnt_ref.1), custom_call_target="tpu_custom_call" | custom-call | tf_op jit(solution)/shard_map/pallas_call | solution.py:209
  74.7 1.9 %broadcast_divide_fusion = f32[64,2048]{1,0:T(8,128)} fusion(f32[64,2048]{1,0:T(8,128)} %get-tuple-element.7, f32[2048]{0:T(1024)} %bitcast.1), kind=kLoop, calls=%fused_computation | loop fusion | flops 131072 | bytes 1056768 | tf_op jit(solution)/shard_map/div | solution.py:231
